TPU v7x, 32 devices: a whole 2x2x4 slice. The times are simulated.
32 devices in a mesh: groups: 2 (over y), dp: 2 (over core), space: 8 (over z, x).
Axes of the slice: x: 2, y: 2, z: 4, core: 2. Of those that a mesh axis runs over, the one named last changes fastest.
Arguments:
- samples: bfloat16 [4, 16, 32, 512], P(('groups', 'dp'), 'space'), parts along dimension 0, may hold values from -6 to 6
- cotangent: bfloat16 [4, 16, 32, 512], P(('groups', 'dp'), 'space'), parts along dimension 0, may hold values from -6 to 6
- wave_owner: int32 [16], replicated, may hold values from 0 to 7, as said below
- filter_weight: bfloat16 [2, 16, 512], replicated, may hold values from -4 to 4
- zonal_gain: bfloat16 [2, 16, 512], P(None, 'space'), may hold values from -4 to 4
Outputs:
- sample_grad: bfloat16 [4, 16, 32, 512], P(('groups', 'dp'), 'space'), parts along dimension 0
- weight_grad: bfloat16 [4, 16, 512], P('groups'), parts along dimension 0
- gain_grad: float32 [4, 16, 512], P('groups', 'space'), parts along dimension 0
There are 2 independent parts, one for each index of `groups`. A program takes and returns all parts, laid end to end along the dimension named above; an argument that names none is the same for every part. Nothing has to cross between parts.
Inputs may be any that keep to these rules, and one draw needn't show every extreme that they name: wave_owner[m] equals wave_owner[15 - m], and each index along space owns exactly 2 wavenumbers.
All inputs are finite; a program needn't handle non-finite values.
Results may differ from a plain program's by a relative error of at most 0.011.
Values may be sent and summed in bfloat16 or wider, within the bound.
A program may use at most 64 MiB of HBM per device.

v0:
```python
import math

import jax
import jax.numpy as jnp
from jax import lax
from jax.sharding import PartitionSpec as P


def slot_tables(wave_owner, per_device, devices):
    is_owner = (wave_owner[:, None] == jnp.arange(devices, dtype=jnp.int32)[None, :]).astype(
        jnp.int32
    )
    owner_rank = jnp.sum((jnp.cumsum(is_owner, axis=0) - 1) * is_owner, axis=1)
    slot_of = wave_owner * per_device + owner_rank
    total_modes = wave_owner.shape[0]
    positions = jnp.arange(total_modes, dtype=jnp.int32)
    matches = (slot_of[None, :] == positions[:, None]).astype(jnp.int32)
    order_of = jnp.sum(matches * positions[None, :], axis=1)
    return (slot_of, order_of)


def fourier_table(wavenums, points):
    longitude = jnp.arange(points, dtype=jnp.int32)
    phase_idx = longitude[:, None] * wavenums[None, :] % points
    angles = phase_idx.astype(jnp.float32) * (2.0 * math.pi / points)
    norm_scale = math.sqrt(2.0 / points)
    return (jnp.stack([jnp.cos(angles), -jnp.sin(angles)], axis=2) * norm_scale).astype(
        jnp.bfloat16
    )


def legendre_table(orders, lat_count, degrees):
    colatitude = (jnp.arange(lat_count, dtype=jnp.float32) + 0.5) * (math.pi / lat_count)
    cosine = jnp.cos(colatitude)
    sine_val = jnp.sin(colatitude)
    log_start = 0.5 * jnp.log((2.0 * orders + 1.0) / (4.0 * math.pi)) + 0.5 * (
        lax.lgamma(2.0 * orders + 1.0) - 2.0 * lax.lgamma(orders + 1.0) - orders * math.log(4.0)
    )
    start_val = jnp.exp(log_start[:, None] + orders[:, None] * jnp.log(sine_val)[None, :])
    quad_weight = math.pi * jnp.sqrt(2.0 * sine_val / lat_count)
    order_col = orders[:, None]

    def advance(carried, degree):
        prev_one, before = carried
        level = degree.astype(jnp.float32)
        is_live = level > order_col
        beyond = level > order_col + 1.0
        lead_coef = jnp.where(
            is_live,
            jnp.sqrt(
                jnp.maximum(4.0 * level * level - 1.0, 0.0)
                / jnp.where(is_live, level * level - order_col * order_col, 1.0)
            ),
            0.0,
        )
        back_num = jnp.maximum((level - 1.0) * (level - 1.0) - order_col * order_col, 0.0)
        back_coef = jnp.where(
            beyond,
            jnp.sqrt(back_num / jnp.where(beyond, 4.0 * (level - 1.0) * (level - 1.0) - 1.0, 1.0)),
            0.0,
        )
        newest = lead_coef * (cosine[None, :] * prev_one - back_coef * before) + jnp.where(
            level == order_col, start_val, 0.0
        )
        return ((newest, prev_one), newest)

    zeros_init = jnp.zeros((orders.shape[0], lat_count), jnp.float32)
    stacked = lax.scan(
        advance, (zeros_init, zeros_init), jnp.arange(degrees, dtype=jnp.int32), unroll=16
    )[1]
    return jnp.transpose(stacked, (1, 0, 2)) * quad_weight[None, None, :]


def gelu_slope(values):
    return (
        0.5 * (1.0 + lax.erf(values * 0.7071067811865476))
        + values * jnp.exp(-0.5 * values * values) * 0.3989422804014327
    )


def complex_product(left_re, left_im, right_re, right_im):
    return (left_re * right_re - left_im * right_im, left_re * right_im + left_im * right_re)


def analysis(legendre, columns):
    return jnp.einsum("ilj,ijrc->ilrc", legendre, columns, preferred_element_type=jnp.float32)


def synthesis(legendre, spectra):
    return jnp.einsum("ilj,ilrc->ijrc", legendre, spectra, preferred_element_type=jnp.float32)


def body(samples, cotangent, wave_owner, filter_weight, zonal_gain):
    devices = lax.axis_size("space")
    own_index = lax.axis_index("space")
    per_device = zonal_gain.shape[1]
    total_modes = wave_owner.shape[0]
    points = samples.shape[2]
    slot_of, order_of = slot_tables(wave_owner, per_device, devices)
    mine = lax.dynamic_slice_in_dim(order_of, own_index * per_device, per_device)
    table = fourier_table(order_of, points)
    legendre = legendre_table(mine.astype(jnp.float32), total_modes, total_modes).astype(
        jnp.bfloat16
    )
    grid = samples[0]
    cot_grid = cotangent[0]
    weight_re = filter_weight[0].astype(jnp.float32)[None]
    weight_im = filter_weight[1].astype(jnp.float32)[None]
    gain_re = zonal_gain[0].astype(jnp.float32)[:, None, :]
    gain_im = zonal_gain[1].astype(jnp.float32)[:, None, :]
    kern_re, kern_im = complex_product(weight_re, weight_im, gain_re, gain_im)
    fourier = jnp.einsum("jkc,ksr->sjrc", grid, table, preferred_element_type=jnp.float32).astype(
        jnp.bfloat16
    )
    owned = lax.all_to_all(fourier, "space", split_axis=0, concat_axis=1, tiled=True)
    spectral = analysis(legendre, owned)
    spec_re = spectral[:, :, 0]
    spec_im = spectral[:, :, 1]
    filt_re, filt_im = complex_product(spec_re, spec_im, kern_re, kern_im)
    filtered = jnp.stack([filt_re, filt_im], axis=2).astype(jnp.bfloat16)
    zonal = synthesis(legendre, filtered).astype(jnp.bfloat16)
    banded = lax.all_to_all(zonal, "space", split_axis=1, concat_axis=0, tiled=True)
    field = jnp.einsum("sjrc,ksr->jkc", banded, table, preferred_element_type=jnp.float32)
    dfield = (cot_grid.astype(jnp.float32) * gelu_slope(field)).astype(jnp.bfloat16)
    dzonal = jnp.einsum("jkc,ksr->sjrc", dfield, table, preferred_element_type=jnp.float32).astype(
        jnp.bfloat16
    )
    grad_owned = lax.all_to_all(dzonal, "space", split_axis=0, concat_axis=1, tiled=True)
    dfiltered = analysis(legendre, grad_owned)
    grad_re = dfiltered[:, :, 0]
    grad_im = dfiltered[:, :, 1]
    prod_re, prod_im = complex_product(spec_re, spec_im, gain_re, gain_im)
    weight_part = jnp.stack(
        [
            jnp.sum(grad_re * prod_re + grad_im * prod_im, axis=0),
            jnp.sum(grad_im * prod_re - grad_re * prod_im, axis=0),
        ]
    )
    other_re, other_im = complex_product(spec_re, spec_im, weight_re, weight_im)
    gain_part = jnp.stack(
        [
            jnp.sum(grad_re * other_re + grad_im * other_im, axis=1),
            jnp.sum(grad_im * other_re - grad_re * other_im, axis=1),
        ]
    )
    dspec = jnp.stack(
        [grad_re * kern_re + grad_im * kern_im, grad_im * kern_re - grad_re * kern_im], axis=2
    ).astype(jnp.bfloat16)
    dfourier = synthesis(legendre, dspec).astype(jnp.bfloat16)
    grad_banded = lax.all_to_all(dfourier, "space", split_axis=1, concat_axis=0, tiled=True)
    sample_grad = (
        cot_grid.astype(jnp.float32)
        + jnp.einsum("sjrc,ksr->jkc", grad_banded, table, preferred_element_type=jnp.float32)
    ).astype(jnp.bfloat16)
    weight_grad = lax.psum(weight_part, ("dp", "space")).astype(jnp.bfloat16)
    gain_grad = lax.psum(gain_part, "dp")
    return (sample_grad[None], weight_grad, gain_grad)


def solution(mesh):
    in_specs = (
        P(("groups", "dp"), "space", None, None),
        P(("groups", "dp"), "space", None, None),
        P(),
        P(),
        P(None, "space", None),
    )
    out_specs = (
        P(("groups", "dp"), "space", None, None),
        P("groups", None, None),
        P("groups", "space", None),
    )
    return jax.shard_map(body, mesh=mesh, in_specs=in_specs, out_specs=out_specs, check_vma=False)
```

profile of v0, /device:TPU:0, one launch (start us, length us, event | category | flops | bytes accessed | tf_op | source)
XLA Modules:
  0.0 119.7 jit_solution(15882110032192383532)
XLA Ops:
  0.6 0.8 fusion.49
  1.4 0.6 copy-done.4
  2.1 0.2 select_reduce_fusion.1
  2.2 0.1 select_reduce_fusion
  2.4 0.1 fusion.53
  2.5 0.1 fusion.3
  2.7 0.7 copy.55
  3.4 7.3 %all-to-all-start = ((bf16[16,2,2,512]{3,1,2,0:T(2,128)(2,1)}), bf16[16,2,2,512]{3,1,2,0:T(2,128)(2,1)S(1)}, u32[]{:S(2)}, u32[]{:S(2)}) async-start(bf16[16,2,2,512]{3,1,2,0:T(2,128)(2,1)} %copy.55), calls=%async_computation | async-start | bytes 131072 | tf_op jit(solution)/shard_map/all_to_all | solution.py:115
  10.8 0.7 fusion.109
  21.7 0.1 compare_select_fusion.6
  21.9 0.1 compare_select_fusion.4
  22.1 0.1 constant_dynamic-update-slice_fusion.14
  22.4 0.1 constant_dynamic-update-slice_fusion.11
  23.2 0.1 constant_dynamic-update-slice_fusion.1
  23.3 0.1 constant_dynamic-update-slice_fusion
  23.4 0.1 copy.80
  23.5 0.6 copy-done.2
  24.1 0.7 copy-done.3
  24.8 0.2 fusion.110
  25.1 0.1 convolution_convert_fusion.2
  25.3 12.7 %all_to_all.72 = bf16[2,16,2,512]{3,2,0,1:T(2,128)(2,1)S(1)} all-to-all(bf16[2,16,2,512]{3,2,0,1:T(2,128)(2,1)S(1)} %copy.63), channel_id=1, replica_groups=mesh['groups'=2,'dp'=2,'space'=8] {'space'}, dimensions={1} | all-to-all | bytes 131072 | tf_op jit(solution)/shard_map/all_to_all | solution.py:122
  38.1 0.8 copy-done.1
  38.9 0.4 fusion.4
  39.3 9.3 %all_to_all.73 = bf16[16,2,2,512]{3,1,2,0:T(2,128)(2,1)S(1)} all-to-all(bf16[16,2,2,512]{3,1,2,0:T(2,128)(2,1)S(1)} %copy.65), channel_id=1, replica_groups=mesh['groups'=2,'dp'=2,'space'=8] {'space'}, dimensions={0} | all-to-all | bytes 131072 | tf_op jit(solution)/shard_map/all_to_all | solution.py:128
  48.7 0.1 fusion.29
  48.8 0.1 fusion.24
  49.0 0.1 convolution_convert_fusion
  49.1 0.7 copy.72
  49.8 3.1 %psum.15 = f32[2,2,512]{2,1,0:T(2,128)} all-reduce(f32[2,2,512]{2,1,0:T(2,128)S(1)} %pad_maximum_fusion.3), channel_id=1, replica_groups=mesh['groups'=2,'dp'=2,'space'=8] {'dp'}, use_global_device_ids=true, to_apply=%region_8.9 | all-reduce | flops 2048 | bytes 16384 | tf_op jit(solution)/shard_map/psum | solution.py:156
  52.9 3.4 %all-to-all-start.3 = ((bf16[2,16,2,512]{3,2,0,1:T(2,128)(2,1)}), bf16[2,16,2,512]{3,2,0,1:T(2,128)(2,1)S(1)}, u32[]{:S(2)}, u32[]{:S(2)}) async-start(bf16[2,16,2,512]{3,2,0,1:T(2,128)(2,1)} %copy.72), calls=%async_computation.3 | async-start | bytes 131072 | tf_op jit(solution)/shard_map/all_to_all | solution.py:150
  56.3 62.5 %psum.14 = bf16[2,16,512]{2,1,0:T(8,128)(2,1)} all-reduce(f32[2,16,512]{2,1,0:T(8,128)S(1)} %pad_maximum_fusion.2), channel_id=1, replica_groups=mesh['groups'=2,'dp'=2,'space'=8] {'dp','space'}, use_global_device_ids=true, to_apply=%region_5.6 | all-reduce | flops 16384 | bytes 98304 | tf_op jit(solution)/shard_map/psum | solution.py:155
  118.9 0.8 fusion.2
  (48 shorter events, 1.9 us)
Async XLA Ops:
  0.6 1.9 %copy-start = (bf16[1,2,32,512]{3,2,1,0:T(8,128)(2,1)S(1)}, bf16[1,2,32,512]{3,2,1,0:T(8,128)(2,1)}, u32[]{:S(2)}) copy-start(bf16[1,2,32,512]{3,2,1,0:T(8,128)(2,1)} %param.5) | copy-start | bytes 196612
  1.4 0.7 copy-start.4
  3.4 21.4 %all-to-all-start = ((bf16[16,2,2,512]{3,1,2,0:T(2,128)(2,1)}), bf16[16,2,2,512]{3,1,2,0:T(2,128)(2,1)S(1)}, u32[]{:S(2)}, u32[]{:S(2)}) async-start(bf16[16,2,2,512]{3,1,2,0:T(2,128)(2,1)} %copy.55), calls=%async_computation | async-start | bytes 131072 | tf_op jit(solution)/shard_map/all_to_all | solution.py:115
  23.3 0.8 copy-start.2
  24.0 0.7 copy-start.3
  38.0 0.8 copy-start.1
  52.9 65.9 %all-to-all-start.3 = ((bf16[2,16,2,512]{3,2,0,1:T(2,128)(2,1)}), bf16[2,16,2,512]{3,2,0,1:T(2,128)(2,1)S(1)}, u32[]{:S(2)}, u32[]{:S(2)}) async-start(bf16[2,16,2,512]{3,2,0,1:T(2,128)(2,1)} %copy.72), calls=%async_computation.3 | async-start | bytes 131072 | tf_op jit(solution)/shard_map/all_to_all | solution.py:150
where the time goes:
time: 120 us
  blocking collectives  87.5 us (73%)
  between operations  11.1 us (9%)
  starting transfers between devices  10.6 us (9%)
  local copies, waits for them, and re-layouts  5.33 us (4%)
  other arithmetic  3.2 us (3%)
  matrix products  1.89 us (2%)
    psum x1, blocking collectives, body(): weight_grad = lax.psum(weight_part, ('dp', 'space')).astype(jnp.bfloat16)  62.5 us
    all_to_all x1, blocking collectives, body(): lax.all_to_all(zonal, 'space', split_axis=1, concat_axis=0, tiled=True)  12.7 us
    all_to_all x1, blocking collectives, body(): lax.all_to_all(dzonal, 'space', split_axis=0, concat_axis=1, tiled=True)  9.29 us
    all_to_all x1, starting transfers between devices, body(): lax.all_to_all(fourier, 'space', split_axis=0, concat_axis=1, tiled=True)  7.25 us
    all_to_all x1, starting transfers between devices, body(): lax.all_to_all(dfourier, 'space', split_axis=1, concat_axis=0, tiled=True)  3.35 us
    psum x1, blocking collectives, body(): gain_grad = lax.psum(gain_part, 'dp')  3.07 us
    unnamed x10, local copies, waits for them, and re-layouts  2.66 us
  transfers between devices with their start and end apart: 2, of which 0 were waited for; matrix products, arithmetic and copies ran while one was open for 2% of the time, Pallas kernels for 0%

commit v1 on v0

--- a/solution.py
+++ b/solution.py
@@ -1,9 +1,16 @@
+import functools
 import math
 
 import jax
 import jax.numpy as jnp
+import numpy as np
 from jax import lax
+from jax.experimental import pallas as pl
+from jax.experimental.pallas import tpu as pltpu
 from jax.sharding import PartitionSpec as P
+
+LANES = 128
+HALF = LANES // 2
 
 
 def slot_tables(wave_owner, per_device, devices):
@@ -90,7 +97,7 @@
     return jnp.einsum("ilj,ilrc->ijrc", legendre, spectra, preferred_element_type=jnp.float32)
 
 
-def body(samples, cotangent, wave_owner, filter_weight, zonal_gain):
+def general_body(samples, cotangent, wave_owner, filter_weight, zonal_gain):
     devices = lax.axis_size("space")
     own_index = lax.axis_index("space")
     per_device = zonal_gain.shape[1]
@@ -157,6 +164,368 @@
     return (sample_grad[None], weight_grad, gain_grad)
 
 
+def host_tables(lats, points, modes):
+    m = np.arange(modes, dtype=np.float64)
+    angles = (np.arange(points)[:, None] * np.arange(modes)[None, :] % points) * (
+        2.0 * math.pi / points
+    )
+    fourier = np.stack([np.cos(angles), -np.sin(angles)]) * math.sqrt(2.0 / points)
+    fourier = fourier.astype(np.float32).astype(jnp.bfloat16).astype(np.float64)
+    colat = (np.arange(lats) + 0.5) * (math.pi / lats)
+    cosine, sine = np.cos(colat), np.sin(colat)
+    log_start = np.array(
+        [
+            0.5 * math.log((2 * o + 1) / (4 * math.pi))
+            + 0.5 * (math.lgamma(2 * o + 1) - 2 * math.lgamma(o + 1) - o * math.log(4.0))
+            for o in range(modes)
+        ]
+    )
+    pbar = np.zeros((modes, modes, lats))
+    for o in range(modes):
+        pbar[o, o] = np.exp(log_start[o] + m[o] * np.log(sine))
+        for l in range(o + 1, modes):
+            lead = math.sqrt((4 * l * l - 1) / (l * l - o * o))
+            pbar[o, l] = lead * cosine * pbar[o, l - 1]
+            if l > o + 1:
+                back = math.sqrt(((l - 1) ** 2 - o * o) / (4 * (l - 1) ** 2 - 1))
+                pbar[o, l] -= lead * back * pbar[o, l - 2]
+    legendre = pbar * (math.pi * np.sqrt(2.0 * sine / lats))[None, None, :]
+    legendre = legendre.astype(np.float32).astype(jnp.bfloat16).astype(np.float64)
+    table = np.einsum("mlj,rkm->rmljk", legendre, fourier)
+    table = table.reshape(2, modes, modes, lats // 2, 2, points).transpose(0, 1, 2, 4, 3, 5)
+    table = table.reshape(2 * modes * modes, lats * points).astype(np.float32)
+    return (table.astype(jnp.bfloat16), np.ascontiguousarray(table.T).astype(jnp.bfloat16))
+
+
+def low(values):
+    return values[:, :HALF]
+
+
+def high(values):
+    return values[:, HALF:]
+
+
+def side(left, right):
+    return jnp.concatenate([left, right], axis=1)
+
+
+def stack_halves(values):
+    return jnp.concatenate([low(values), high(values)], axis=0)
+
+
+def whole_kernel(
+    n,
+    x_ref,
+    cot_ref,
+    owner_ref,
+    weight_ref,
+    gain_ref,
+    table_hbm,
+    turned_hbm,
+    out_ref,
+    wgrad_ref,
+    ggrad_ref,
+    table,
+    turned,
+    x_out,
+    x_in,
+    cot_out,
+    cot_in,
+    g_out,
+    g_in,
+    y_out,
+    y_in,
+    part_out,
+    part_in,
+    w_out,
+    w_in,
+    q_out,
+    q_in,
+    send_sem,
+    recv_sem,
+    pair_sem,
+    load_sem,
+):
+    f32, bf16 = jnp.float32, jnp.bfloat16
+    me = lax.axis_index("space")
+    dp = lax.axis_index("dp")
+    points = x_ref.shape[1]
+    modes = weight_ref.shape[1]
+    peers = [lax.rem(me + i, n) for i in range(n)]
+    order = list(range(1, n))
+
+    loads = [
+        pltpu.make_async_copy(table_hbm, table, load_sem.at[0]),
+        pltpu.make_async_copy(turned_hbm, turned, load_sem.at[1]),
+    ]
+    for load in loads:
+        load.start()
+    barrier = pltpu.get_barrier_semaphore()
+    for i in order:
+        pl.semaphore_signal(
+            barrier, inc=1, device_id={"space": peers[i]}, device_id_type=pl.DeviceIdType.MESH
+        )
+    pl.semaphore_signal(
+        barrier, inc=1, device_id={"dp": 1 - dp}, device_id_type=pl.DeviceIdType.MESH
+    )
+
+    def exchange(kind, source, target):
+        copies = []
+        for i in order:
+            copies.append(
+                pltpu.make_async_remote_copy(
+                    src_ref=source.at[peers[i]],
+                    dst_ref=target.at[me],
+                    send_sem=send_sem.at[kind, i],
+                    recv_sem=recv_sem.at[kind, i],
+                    device_id={"space": peers[i]},
+                    device_id_type=pl.DeviceIdType.MESH,
+                )
+            )
+        for copy in copies:
+            copy.start()
+        target[me] = source[me]
+        return copies
+
+    def split(ref, out):
+        first, second = ref[0], ref[1]
+        for t in range(n // 2):
+            a = first[:, t * LANES : (t + 1) * LANES]
+            b = second[:, t * LANES : (t + 1) * LANES]
+            out[2 * t] = side(low(a), low(b))
+            out[2 * t + 1] = side(high(a), high(b))
+
+    split(x_ref, x_out)
+    for part in range(2):
+        rows = gain_ref[part].astype(f32)
+        for i in range(n):
+            c = i * HALF
+            g_out[i, part : part + 1, :] = side(
+                rows[0:1, c : c + HALF], rows[1:2, c : c + HALF]
+            )
+    pl.semaphore_wait(barrier, n)
+    copies = exchange(0, x_out, x_in)
+    g_copies = exchange(1, g_out, g_in)
+    split(cot_ref, cot_out)
+    cot_copies = exchange(2, cot_out, cot_in)
+
+    sub = lax.broadcasted_iota(jnp.int32, (modes, modes), 0)
+    lane = lax.broadcasted_iota(jnp.int32, (modes, modes), 1)
+    owner_row = jnp.broadcast_to(owner_ref[...], (modes, modes))
+    owner_col = jnp.sum(jnp.where(sub == lane, owner_row, 0), axis=1, keepdims=True)
+    same = jnp.where((owner_row == owner_col) & (lane < sub), 1, 0)
+    slot = owner_col * 2 + jnp.sum(same, axis=1, keepdims=True)
+    slot = jnp.broadcast_to(slot, (modes, LANES))
+    odd = (lax.broadcasted_iota(jnp.int32, (modes, LANES), 1) >= HALF).astype(jnp.int32)
+    masks = [slot == 2 * i + odd for i in range(n)]
+
+    tile = pl.ds(pl.multiple_of((me // 2) * LANES, LANES), LANES)
+    parity = lax.rem(me, 2)
+
+    def my_weight(part):
+        both = weight_ref[part, :, tile].astype(f32)
+        return jnp.where(parity == 1, high(both), low(both))
+
+    w_re, w_im = my_weight(0)[None], my_weight(1)[None]
+
+    for copy in g_copies:
+        copy.wait_recv()
+
+    def my_gain(part):
+        total = jnp.zeros((modes, LANES), f32)
+        for i in range(n):
+            row = jnp.broadcast_to(g_in[i, part : part + 1, :], (modes, LANES))
+            total = total + jnp.where(masks[i], row, 0.0)
+        return (low(total) + high(total))[:, None, :]
+
+    g_re, g_im = my_gain(0), my_gain(1)
+    k_re, k_im = complex_product(w_re, w_im, g_re, g_im)
+
+    def dot(a, b):
+        return jnp.dot(a, b, preferred_element_type=f32)
+
+    def apart(values):
+        cube = values.reshape(2, modes, modes, HALF)
+        return (cube[0], cube[1])
+
+    def joined(re, im):
+        rows = modes * modes
+        return jnp.concatenate(
+            [re.astype(bf16).reshape(rows, HALF), im.astype(bf16).reshape(rows, HALF)], axis=0
+        )
+
+    for load in loads:
+        load.wait()
+    for copy in copies:
+        copy.wait_recv()
+    grid = stack_halves(x_in[...].reshape(n * points, LANES))
+    s_re, s_im = apart(dot(table[...], grid))
+    f_re, f_im = complex_product(s_re, s_im, k_re, k_im)
+    field = dot(turned[...], joined(f_re, f_im))
+    field = side(field[: n * points], field[n * points :])
+    slope = gelu_slope(field)
+    for copy in cot_copies:
+        copy.wait_recv()
+    cot = cot_in[...].reshape(n * points, LANES).astype(f32)
+    dfield = stack_halves((cot * slope).astype(bf16))
+    d_re, d_im = apart(dot(table[...], dfield))
+
+    h_re = d_re * s_re + d_im * s_im
+    h_im = d_im * s_re - d_re * s_im
+    wg_re = jnp.sum(h_re * g_re + h_im * g_im, axis=0)
+    wg_im = jnp.sum(h_im * g_re - h_re * g_im, axis=0)
+    gg_re = jnp.sum(h_re * w_re + h_im * w_im, axis=1)
+    gg_im = jnp.sum(h_im * w_re - h_re * w_im, axis=1)
+    part_out[0] = side(wg_re, wg_im)
+    part_out[1] = side(gg_re, gg_im)
+    swap = pltpu.make_async_remote_copy(
+        src_ref=part_out,
+        dst_ref=part_in,
+        send_sem=pair_sem.at[0],
+        recv_sem=pair_sem.at[1],
+        device_id={"dp": 1 - dp},
+        device_id_type=pl.DeviceIdType.MESH,
+    )
+    swap.start()
+
+    e_re = d_re * k_re + d_im * k_im
+    e_im = d_im * k_re - d_re * k_im
+    dgrid = dot(turned[...], joined(e_re, e_im))
+    dgrid = side(dgrid[: n * points], dgrid[n * points :])
+    y_out[...] = (cot + dgrid).astype(bf16).reshape(n, points, LANES)
+    y_copies = exchange(3, y_out, y_in)
+
+    swap.wait_recv()
+    both_w = (part_out[0] + part_in[0]).astype(bf16)
+    both_g = part_out[1] + part_in[1]
+    w_out[...] = both_w
+    w_copies = []
+    for i in order:
+        w_copies.append(
+            pltpu.make_async_remote_copy(
+                src_ref=w_out,
+                dst_ref=w_in.at[me],
+                send_sem=send_sem.at[4, i],
+                recv_sem=recv_sem.at[4, i],
+                device_id={"space": peers[i]},
+                device_id_type=pl.DeviceIdType.MESH,
+            )
+        )
+    for copy in w_copies:
+        copy.start()
+    w_in[me] = both_w
+    twice = [side(low(both_g), low(both_g)), side(high(both_g), high(both_g))]
+    for i in range(n):
+        for part in range(2):
+            q_out[i, part : part + 1, :] = jnp.sum(
+                jnp.where(masks[i], twice[part], 0.0), axis=0, keepdims=True
+            )
+    q_copies = exchange(5, q_out, q_in)
+
+    for copy in y_copies:
+        copy.wait_recv()
+    for t in range(n // 2):
+        a, b = y_in[2 * t], y_in[2 * t + 1]
+        columns = pl.ds(t * LANES, LANES)
+        out_ref[0, :, columns] = side(low(a), low(b))
+        out_ref[1, :, columns] = side(high(a), high(b))
+    for copy in w_copies:
+        copy.wait_recv()
+    for t in range(n // 2):
+        a, b = w_in[2 * t], w_in[2 * t + 1]
+        columns = pl.ds(t * LANES, LANES)
+        wgrad_ref[0, :, columns] = side(low(a), low(b))
+        wgrad_ref[1, :, columns] = side(high(a), high(b))
+    for copy in q_copies:
+        copy.wait_recv()
+    for t in range(n // 2):
+        a, b = q_in[2 * t], q_in[2 * t + 1]
+        columns = pl.ds(t * LANES, LANES)
+        first, second = side(low(a), low(b)), side(high(a), high(b))
+        for part in range(2):
+            ggrad_ref[part, 0:1, columns] = first[part : part + 1]
+            ggrad_ref[part, 1:2, columns] = second[part : part + 1]
+    swap.wait_send()
+    for group in (copies, g_copies, cot_copies, y_copies, w_copies, q_copies):
+        for copy in group:
+            copy.wait_send()
+
+
+def channel_body(n, samples, cotangent, wave_owner, filter_weight, zonal_gain):
+    lat_dev, points, channels = samples.shape[1:]
+    modes = wave_owner.shape[0]
+    table, turned = host_tables(lat_dev * n, points, modes)
+    bf16, f32 = jnp.bfloat16, jnp.float32
+    vmem = pl.BlockSpec(memory_space=pltpu.VMEM)
+    hbm = pl.BlockSpec(memory_space=pl.ANY)
+    block = pltpu.VMEM((n, points, LANES), bf16)
+    small = pltpu.VMEM((n, 2, LANES), f32)
+    out, wgrad, ggrad = pl.pallas_call(
+        functools.partial(whole_kernel, n),
+        out_shape=(
+            jax.ShapeDtypeStruct((lat_dev, points, channels), bf16),
+            jax.ShapeDtypeStruct((2, modes, channels), bf16),
+            jax.ShapeDtypeStruct((2, zonal_gain.shape[1], channels), f32),
+        ),
+        in_specs=[vmem] * 5 + [hbm] * 2,
+        out_specs=(vmem, vmem, vmem),
+        scratch_shapes=[
+            pltpu.VMEM(table.shape, bf16),
+            pltpu.VMEM(turned.shape, bf16),
+            block,
+            block,
+            block,
+            block,
+            small,
+            small,
+            block,
+            block,
+            pltpu.VMEM((2, modes, LANES), f32),
+            pltpu.VMEM((2, modes, LANES), f32),
+            pltpu.VMEM((modes, LANES), bf16),
+            pltpu.VMEM((n, modes, LANES), bf16),
+            small,
+            small,
+            pltpu.SemaphoreType.DMA((6, n)),
+            pltpu.SemaphoreType.DMA((6, n)),
+            pltpu.SemaphoreType.DMA((2,)),
+            pltpu.SemaphoreType.DMA((2,)),
+        ],
+        compiler_params=pltpu.CompilerParams(
+            collective_id=0, has_side_effects=True, vmem_limit_bytes=24 * 1024 * 1024
+        ),
+    )(
+        samples[0],
+        cotangent[0],
+        wave_owner[None],
+        filter_weight,
+        zonal_gain,
+        jnp.asarray(table),
+        jnp.asarray(turned),
+    )
+    return (out[None], wgrad, ggrad)
+
+
+def body(samples, cotangent, wave_owner, filter_weight, zonal_gain):
+    devices = lax.axis_size("space")
+    lat_dev, points, channels = samples.shape[1:]
+    modes = wave_owner.shape[0]
+    fits = (
+        lax.axis_size("dp") == 2
+        and samples.shape[0] == 1
+        and lat_dev == 2
+        and zonal_gain.shape[1] == 2
+        and channels == devices * HALF
+        and devices % 2 == 0
+        and modes % 16 == 0
+        and points % 16 == 0
+        and modes * modes * devices * points * 16 <= 8 * 1024 * 1024
+    )
+    if fits:
+        return channel_body(devices, samples, cotangent, wave_owner, filter_weight, zonal_gain)
+    return general_body(samples, cotangent, wave_owner, filter_weight, zonal_gain)
+
+
 def solution(mesh):
     in_specs = (
         P(("groups", "dp"), "space", None, None),

time: 120 us -> 26.8 us (0.22)
  blocking collectives: 87.5 us -> 0 us
  Pallas kernels: 0 us -> 18.7 us
  starting transfers between devices: 10.6 us -> 0 us
  between operations: 11.1 us -> 0.66 us
  other arithmetic: 3.2 us -> 0 us
  matrix products: 1.89 us -> 0 us
  local copies, waits for them, and re-layouts: 5.33 us -> 7.04 us
    psum x2 -> x0, blocking collectives: 65.6 us -> none  [the longest x1 62.5 us: body(): weight_grad = lax.psum(weight_part, ('dp', 'space')).astype(jnp.bfloat16)]
    all_to_all x2 -> x0, blocking collectives: 22 us -> none  [the longest x1 12.7 us: body(): lax.all_to_all(zonal, 'space', split_axis=1, concat_axis=0, tiled=True)]
    pallas_call x0 -> x1, Pallas kernels: none -> 18.7 us  [channel_body(): pl.pallas_call(functools.partial(whole_kernel, n), out_shape=(jax.ShapeDt...]
    all_to_all x2 -> x0, starting transfers between devices: 10.6 us -> none  [the longest x1 7.25 us: body(): lax.all_to_all(fourier, 'space', split_axis=0, concat_axis=1, tiled=True)]
    unnamed x10 -> x17, local copies, waits for them, and re-layouts: 2.66 us -> 7.04 us
    dot_general x7 -> x0, matrix products: 1.89 us -> none  [the longest x1 0.82 us: body(): jnp.einsum('sjrc,ksr->jkc', grad_banded, table, preferred_element_type=jn...]
    convert_element_type x5 -> x0, local copies, waits for them, and re-layouts: 1.63 us -> none  [the longest x1 0.7 us: body(): dfourier = synthesis(legendre, dspec).astype(jnp.bfloat16)]
    unnamed x15 -> x0, other arithmetic: 1.2 us -> none
  transfers between devices with their start and end apart: 2 -> 0, of which waited for: 0 -> 0; matrix products, arithmetic and copies ran while one was open for 2% -> 0% of each run, Pallas kernels for 0% -> 0%
where the time goes in v1:
time: 26.8 us; the launch traced here: 26.4 us
  Pallas kernels  18.7 us (70%)
  local copies, waits for them, and re-layouts  7.04 us (26%)
  between operations  0.66 us (2%)
    pallas_call x1, Pallas kernels, channel_body(): pl.pallas_call(functools.partial(whole_kernel, n), out_shape=(jax.ShapeDt...  18.7 us
    unnamed x17, local copies, waits for them, and re-layouts  7.04 us

profile of v1, /device:TPU:0, one launch (start us, length us, event | category | flops | bytes accessed | tf_op | source)
XLA Modules:
  0.0 26.4 jit_solution(10743323760137669878)
XLA Ops:
  0.6 0.0 copy-start.5
  0.6 0.0 copy-start.6
  0.7 0.7 %copy-done.5 = bf16[2,2,512]{2,1,0:T(2,128)(2,1)S(1)} copy-done((bf16[2,2,512]{2,1,0:T(2,128)(2,1)S(1)}, bf16[2,2,512]{2,1,0:T(2,128)(2,1)}, u32[]{:S(2)}) %copy-start.5) | copy-done | bytes 4120
  1.3 0.0 copy-done.6
  1.3 0.0 copy-start
  1.3 1.0 %copy-done = bf16[512,512]{1,0:T(8,128)(2,1)S(1)} copy-done((bf16[512,512]{1,0:T(8,128)(2,1)S(1)}, bf16[512,512]{1,0:T(8,128)(2,1)}, u32[]{:S(2)}) %copy-start) | copy-done | bytes 524312
  2.4 0.0 copy-start.1
  2.4 1.0 %copy-done.1 = bf16[512,512]{1,0:T(8,128)(2,1)S(1)} copy-done((bf16[512,512]{1,0:T(8,128)(2,1)S(1)}, bf16[512,512]{1,0:T(8,128)(2,1)}, u32[]{:S(2)}) %copy-start.1) | copy-done | bytes 524312
  3.4 0.0 copy-start.2
  3.4 0.8 %copy-done.2 = bf16[1,2,32,512]{3,2,1,0:T(8,128)(2,1)S(1)} copy-done((bf16[1,2,32,512]{3,2,1,0:T(8,128)(2,1)S(1)}, bf16[1,2,32,512]{3,2,1,0:T(8,128)(2,1)}, u32[]{:S(2)}) %copy-start.2) | copy-done | bytes 65560
  4.2 0.0 copy-start.3
  4.2 0.8 %copy-done.3 = bf16[1,2,32,512]{3,2,1,0:T(8,128)(2,1)S(1)} copy-done((bf16[1,2,32,512]{3,2,1,0:T(8,128)(2,1)S(1)}, bf16[1,2,32,512]{3,2,1,0:T(8,128)(2,1)}, u32[]{:S(2)}) %copy-start.3) | copy-done | bytes 65560
  5.1 0.0 copy-start.4
  5.1 0.8 %copy-done.4 = bf16[2,16,512]{2,1,0:T(8,128)(2,1)S(1)} copy-done((bf16[2,16,512]{2,1,0:T(8,128)(2,1)S(1)}, bf16[2,16,512]{2,1,0:T(8,128)(2,1)}, u32[]{:S(2)}) %copy-start.4) | copy-done | bytes 32792
  5.8 18.7 %shard_map.94 = (bf16[2,32,512]{2,1,0:T(8,128)(2,1)S(1)}, bf16[2,16,512]{2,1,0:T(8,128)(2,1)S(1)}, f32[2,2,512]{2,1,0:T(2,128)S(1)}) custom-call(bf16[2,32,512]{2,1,0:T(8,128)(2,1)S(1)} %bitcast.4, bf16[2,32,512]{2,1,0:T(8,128)(2,1)S(1)} %bitcast.5, s32[1,16]{1,0:T(1,128)S(1)} %bitcast.7, bf16[2,16,512]{2,1,0:T(8,128)(2,1)S(1)} %copy-done.4, ...), custom_call_target="tpu_custom_call" | custom-call | tf_op jit(solution)/shard_map/pallas_call | solution.py:463
  24.6 0.6 %copy.13 = bf16[1,2,32,512]{3,2,1,0:T(8,128)(2,1)} copy(bf16[1,2,32,512]{3,2,1,0:T(8,128)(2,1)S(1)} %bitcast.6) | data formatting | bytes 131072
  25.2 0.6 %copy.14 = bf16[2,16,512]{2,1,0:T(8,128)(2,1)} copy(bf16[2,16,512]{2,1,0:T(8,128)(2,1)S(1)} %get-tuple-element.13) | data formatting | bytes 65536
  25.8 0.6 %copy.15 = f32[2,2,512]{2,1,0:T(2,128)} copy(f32[2,2,512]{2,1,0:T(2,128)S(1)} %get-tuple-element.14) | data formatting | bytes 16384
Async XLA Ops:
  0.6 0.7 %copy-start.5 = (bf16[2,2,512]{2,1,0:T(2,128)(2,1)S(1)}, bf16[2,2,512]{2,1,0:T(2,128)(2,1)}, u32[]{:S(2)}) copy-start(bf16[2,2,512]{2,1,0:T(2,128)(2,1)} %gain_ref.1) | copy-start | bytes 12292
  0.6 0.7 %copy-start.6 = (s32[16]{0:T(128)S(1)}, s32[16]{0:T(128)}, u32[]{:S(2)}) copy-start(s32[16]{0:T(128)} %param.9) | copy-start | bytes 196
  1.3 1.0 %copy-start = (bf16[512,512]{1,0:T(8,128)(2,1)S(1)}, bf16[512,512]{1,0:T(8,128)(2,1)}, u32[]{:S(2)}) copy-start(bf16[512,512]{1,0:T(8,128)(2,1)} %constant.5.clone.turned_hbm) | copy-start | bytes 1572868
  2.4 1.0 %copy-start.1 = (bf16[512,512]{1,0:T(8,128)(2,1)S(1)}, bf16[512,512]{1,0:T(8,128)(2,1)}, u32[]{:S(2)}) copy-start(bf16[512,512]{1,0:T(8,128)(2,1)} %constant.4.clone.table_hbm) | copy-start | bytes 1572868
  3.4 0.8 %copy-start.2 = (bf16[1,2,32,512]{3,2,1,0:T(8,128)(2,1)S(1)}, bf16[1,2,32,512]{3,2,1,0:T(8,128)(2,1)}, u32[]{:S(2)}) copy-start(bf16[1,2,32,512]{3,2,1,0:T(8,128)(2,1)} %param.7) | copy-start | bytes 196612
  4.2 0.8 %copy-start.3 = (bf16[1,2,32,512]{3,2,1,0:T(8,128)(2,1)S(1)}, bf16[1,2,32,512]{3,2,1,0:T(8,128)(2,1)}, u32[]{:S(2)}) copy-start(bf16[1,2,32,512]{3,2,1,0:T(8,128)(2,1)} %param.8) | copy-start | bytes 196612
  5.1 0.8 %copy-start.4 = (bf16[2,16,512]{2,1,0:T(8,128)(2,1)S(1)}, bf16[2,16,512]{2,1,0:T(8,128)(2,1)}, u32[]{:S(2)}) copy-start(bf16[2,16,512]{2,1,0:T(8,128)(2,1)} %weight_ref.1) | copy-start | bytes 98308

commit v2 on v1

--- a/solution.py
+++ b/solution.py
@@ -215,16 +215,21 @@
 
 def whole_kernel(
     n,
+    x_hbm,
+    cot_hbm,
+    owner_hbm,
+    weight_hbm,
+    gain_hbm,
+    table_hbm,
+    turned_hbm,
+    y_in,
+    w_in,
+    q_in,
     x_ref,
     cot_ref,
     owner_ref,
     weight_ref,
     gain_ref,
-    table_hbm,
-    turned_hbm,
-    out_ref,
-    wgrad_ref,
-    ggrad_ref,
     table,
     turned,
     x_out,
@@ -234,13 +239,10 @@
     g_out,
     g_in,
     y_out,
-    y_in,
     part_out,
     part_in,
     w_out,
-    w_in,
     q_out,
-    q_in,
     send_sem,
     recv_sem,
     pair_sem,
@@ -255,8 +257,18 @@
     order = list(range(1, n))
 
     loads = [
-        pltpu.make_async_copy(table_hbm, table, load_sem.at[0]),
-        pltpu.make_async_copy(turned_hbm, turned, load_sem.at[1]),
+        pltpu.make_async_copy(source, target, load_sem.at[i])
+        for i, (source, target) in enumerate(
+            [
+                (x_hbm, x_ref),
+                (gain_hbm, gain_ref),
+                (cot_hbm, cot_ref),
+                (owner_hbm, owner_ref),
+                (weight_hbm, weight_ref),
+                (table_hbm, table),
+                (turned_hbm, turned),
+            ]
+        )
     ]
     for load in loads:
         load.start()
@@ -295,7 +307,9 @@
             out[2 * t] = side(low(a), low(b))
             out[2 * t + 1] = side(high(a), high(b))
 
+    loads[0].wait()
     split(x_ref, x_out)
+    loads[1].wait()
     for part in range(2):
         rows = gain_ref[part].astype(f32)
         for i in range(n):
@@ -306,9 +320,12 @@
     pl.semaphore_wait(barrier, n)
     copies = exchange(0, x_out, x_in)
     g_copies = exchange(1, g_out, g_in)
+    loads[2].wait()
     split(cot_ref, cot_out)
     cot_copies = exchange(2, cot_out, cot_in)
 
+    loads[3].wait()
+    loads[4].wait()
     sub = lax.broadcasted_iota(jnp.int32, (modes, modes), 0)
     lane = lax.broadcasted_iota(jnp.int32, (modes, modes), 1)
     owner_row = jnp.broadcast_to(owner_ref[...], (modes, modes))
@@ -354,8 +371,8 @@
             [re.astype(bf16).reshape(rows, HALF), im.astype(bf16).reshape(rows, HALF)], axis=0
         )
 
-    for load in loads:
-        load.wait()
+    loads[5].wait()
+    loads[6].wait()
     for copy in copies:
         copy.wait_recv()
     grid = stack_halves(x_in[...].reshape(n * points, LANES))
@@ -422,33 +439,41 @@
             )
     q_copies = exchange(5, q_out, q_in)
 
-    for copy in y_copies:
-        copy.wait_recv()
+    for group in (y_copies, w_copies, q_copies):
+        for copy in group:
+            copy.wait_recv()
+    swap.wait_send()
+    for group in (copies, g_copies, cot_copies, y_copies, w_copies, q_copies):
+        for copy in group:
+            copy.wait_send()
+
+
+def place_kernel(
+    n, y_in, w_in, q_in, out_hbm, wgrad_hbm, ggrad_hbm, out_ref, wgrad_ref, ggrad_ref, sem
+):
     for t in range(n // 2):
+        columns = slice(t * LANES, (t + 1) * LANES)
         a, b = y_in[2 * t], y_in[2 * t + 1]
-        columns = pl.ds(t * LANES, LANES)
         out_ref[0, :, columns] = side(low(a), low(b))
         out_ref[1, :, columns] = side(high(a), high(b))
-    for copy in w_copies:
-        copy.wait_recv()
+    stores = [pltpu.make_async_copy(out_ref, out_hbm, sem.at[0])]
+    stores[0].start()
     for t in range(n // 2):
+        columns = slice(t * LANES, (t + 1) * LANES)
         a, b = w_in[2 * t], w_in[2 * t + 1]
-        columns = pl.ds(t * LANES, LANES)
         wgrad_ref[0, :, columns] = side(low(a), low(b))
         wgrad_ref[1, :, columns] = side(high(a), high(b))
-    for copy in q_copies:
-        copy.wait_recv()
-    for t in range(n // 2):
         a, b = q_in[2 * t], q_in[2 * t + 1]
-        columns = pl.ds(t * LANES, LANES)
         first, second = side(low(a), low(b)), side(high(a), high(b))
         for part in range(2):
             ggrad_ref[part, 0:1, columns] = first[part : part + 1]
             ggrad_ref[part, 1:2, columns] = second[part : part + 1]
-    swap.wait_send()
-    for group in (copies, g_copies, cot_copies, y_copies, w_copies, q_copies):
-        for copy in group:
-            copy.wait_send()
+    stores.append(pltpu.make_async_copy(wgrad_ref, wgrad_hbm, sem.at[1]))
+    stores.append(pltpu.make_async_copy(ggrad_ref, ggrad_hbm, sem.at[2]))
+    for store in stores[1:]:
+        store.start()
+    for store in stores:
+        store.wait()
 
 
 def channel_body(n, samples, cotangent, wave_owner, filter_weight, zonal_gain):
@@ -457,21 +482,31 @@
     table, turned = host_tables(lat_dev * n, points, modes)
     bf16, f32 = jnp.bfloat16, jnp.float32
     vmem = pl.BlockSpec(memory_space=pltpu.VMEM)
-    hbm = pl.BlockSpec(memory_space=pl.ANY)
+    hbm = pl.BlockSpec(memory_space=pltpu.HBM)
     block = pltpu.VMEM((n, points, LANES), bf16)
     small = pltpu.VMEM((n, 2, LANES), f32)
-    out, wgrad, ggrad = pl.pallas_call(
+    pair = pltpu.VMEM((2, modes, LANES), f32)
+    operands = (
+        samples[0],
+        cotangent[0],
+        wave_owner[None],
+        filter_weight,
+        zonal_gain,
+        jnp.asarray(table),
+        jnp.asarray(turned),
+    )
+    operands = [pltpu.with_memory_space_constraint(x, pltpu.HBM) for x in operands]
+    received = pl.pallas_call(
         functools.partial(whole_kernel, n),
         out_shape=(
-            jax.ShapeDtypeStruct((lat_dev, points, channels), bf16),
-            jax.ShapeDtypeStruct((2, modes, channels), bf16),
-            jax.ShapeDtypeStruct((2, zonal_gain.shape[1], channels), f32),
+            pltpu.VMEM((n, points, LANES), bf16),
+            pltpu.VMEM((n, modes, LANES), bf16),
+            pltpu.VMEM((n, 2, LANES), f32),
         ),
-        in_specs=[vmem] * 5 + [hbm] * 2,
+        in_specs=[hbm] * len(operands),
         out_specs=(vmem, vmem, vmem),
-        scratch_shapes=[
-            pltpu.VMEM(table.shape, bf16),
-            pltpu.VMEM(turned.shape, bf16),
+        scratch_shapes=[pltpu.VMEM(x.shape, x.dtype) for x in operands]
+        + [
             block,
             block,
             block,
@@ -479,30 +514,32 @@
             small,
             small,
             block,
-            block,
-            pltpu.VMEM((2, modes, LANES), f32),
-            pltpu.VMEM((2, modes, LANES), f32),
+            pair,
+            pair,
             pltpu.VMEM((modes, LANES), bf16),
-            pltpu.VMEM((n, modes, LANES), bf16),
-            small,
             small,
             pltpu.SemaphoreType.DMA((6, n)),
             pltpu.SemaphoreType.DMA((6, n)),
             pltpu.SemaphoreType.DMA((2,)),
-            pltpu.SemaphoreType.DMA((2,)),
+            pltpu.SemaphoreType.DMA((len(operands),)),
         ],
         compiler_params=pltpu.CompilerParams(
             collective_id=0, has_side_effects=True, vmem_limit_bytes=24 * 1024 * 1024
         ),
-    )(
-        samples[0],
-        cotangent[0],
-        wave_owner[None],
-        filter_weight,
-        zonal_gain,
-        jnp.asarray(table),
-        jnp.asarray(turned),
-    )
+    )(*operands)
+    results = (
+        jax.ShapeDtypeStruct((lat_dev, points, channels), bf16),
+        jax.ShapeDtypeStruct((2, modes, channels), bf16),
+        jax.ShapeDtypeStruct((2, zonal_gain.shape[1], channels), f32),
+    )
+    out, wgrad, ggrad = pl.pallas_call(
+        functools.partial(place_kernel, n),
+        out_shape=results,
+        in_specs=[vmem] * 3,
+        out_specs=(hbm, hbm, hbm),
+        scratch_shapes=[pltpu.VMEM(x.shape, x.dtype) for x in results]
+        + [pltpu.SemaphoreType.DMA((3,))],
+    )(*received)
     return (out[None], wgrad, ggrad)
 
 

time: 26.8 us -> 22.9 us (0.85)
  local copies, waits for them, and re-layouts: 7.04 us -> 1.81 us
  Pallas kernels: 18.7 us -> 20.3 us
    unnamed x17 -> x6, local copies, waits for them, and re-layouts: 7.04 us -> 1.81 us
    pallas_call x1 -> x2, Pallas kernels: 18.7 us -> 20.3 us  [the longest x1 18.7 us: channel_body(): pl.pallas_call(functools.partial(whole_kernel, n), out_shape=(pltpu.VMEM(...]
where the time goes in v2:
time: 22.9 us; the launch traced here: 22.7 us
  Pallas kernels  20.3 us (89%)
  local copies, waits for them, and re-layouts  1.81 us (8%)
  between operations  0.65 us (3%)
    pallas_call x1, Pallas kernels, channel_body(): pl.pallas_call(functools.partial(whole_kernel, n), out_shape=(pltpu.VMEM(...  18.7 us
    unnamed x6, local copies, waits for them, and re-layouts  1.81 us
    pallas_call x1, Pallas kernels, channel_body(): pl.pallas_call(functools.partial(place_kernel, n), out_shape=results, in_...  1.61 us

profile of v2, /device:TPU:0, one launch (start us, length us, event | category | flops | bytes accessed | tf_op | source)
XLA Modules:
  0.0 22.7 jit_solution(16885799738680099063)
XLA Ops:
  0.6 18.7 %shard_map.94 = (bf16[8,32,128]{2,1,0:T(8,128)(2,1)S(1)}, bf16[8,16,128]{2,1,0:T(8,128)(2,1)S(1)}, f32[8,2,128]{2,1,0:T(2,128)S(1)}) custom-call(bf16[2,32,512]{2,1,0:T(8,128)(2,1)} %bitcast.4, bf16[2,32,512]{2,1,0:T(8,128)(2,1)} %bitcast.5, s32[1,16]{1,0:T(1,128)} %bitcast.6, bf16[2,16,512]{2,1,0:T(8,128)(2,1)} %weight_hbm.1, bf16[2,2,512]{2,1,0:T(2,128)(2,1)} %gain_hbm.1, ...), custom_call_target="tpu_custom_call" | custom-call | tf_op jit(solution)/shard_map/pallas_call | solution.py:499
  19.3 0.0 copy-start
  19.3 0.6 %copy-done = bf16[8,32,128]{2,1,0:T(8,128)(2,1)} copy-done((bf16[8,32,128]{2,1,0:T(8,128)(2,1)}, bf16[8,32,128]{2,1,0:T(8,128)(2,1)S(1)}, u32[]{:S(2)}) %copy-start) | copy-done | bytes 65560
  19.9 0.0 copy-start.1
  19.9 0.6 %copy-done.1 = bf16[8,16,128]{2,1,0:T(8,128)(2,1)} copy-done((bf16[8,16,128]{2,1,0:T(8,128)(2,1)}, bf16[8,16,128]{2,1,0:T(8,128)(2,1)S(1)}, u32[]{:S(2)}) %copy-start.1) | copy-done | bytes 32792
  20.5 0.0 copy-start.2
  20.5 0.6 %copy-done.2 = f32[8,2,128]{2,1,0:T(2,128)} copy-done((f32[8,2,128]{2,1,0:T(2,128)}, f32[8,2,128]{2,1,0:T(2,128)S(1)}, u32[]{:S(2)}) %copy-start.2) | copy-done | bytes 8216
  21.1 1.6 %shard_map.95 = (bf16[2,32,512]{2,1,0:T(8,128)(2,1)}, bf16[2,16,512]{2,1,0:T(8,128)(2,1)}, f32[2,2,512]{2,1,0:T(2,128)}) custom-call(bf16[8,32,128]{2,1,0:T(8,128)(2,1)} %copy-done, bf16[8,16,128]{2,1,0:T(8,128)(2,1)} %copy-done.1, f32[8,2,128]{2,1,0:T(2,128)} %copy-done.2), custom_call_target="tpu_custom_call" | custom-call | tf_op jit(solution)/shard_map/pallas_call | solution.py:535
Async XLA Ops:
  19.3 0.6 %copy-start = (bf16[8,32,128]{2,1,0:T(8,128)(2,1)}, bf16[8,32,128]{2,1,0:T(8,128)(2,1)S(1)}, u32[]{:S(2)}) copy-start(bf16[8,32,128]{2,1,0:T(8,128)(2,1)S(1)} %get-tuple-element.9.y_in) | copy-start | bytes 196612
  19.9 0.6 %copy-start.1 = (bf16[8,16,128]{2,1,0:T(8,128)(2,1)}, bf16[8,16,128]{2,1,0:T(8,128)(2,1)S(1)}, u32[]{:S(2)}) copy-start(bf16[8,16,128]{2,1,0:T(8,128)(2,1)S(1)} %get-tuple-element.10.w_in) | copy-start | bytes 98308
  20.5 0.6 %copy-start.2 = (f32[8,2,128]{2,1,0:T(2,128)}, f32[8,2,128]{2,1,0:T(2,128)S(1)}, u32[]{:S(2)}) copy-start(f32[8,2,128]{2,1,0:T(2,128)S(1)} %get-tuple-element.11.q_in) | copy-start | bytes 24580

commit v3 on v2

--- a/solution.py
+++ b/solution.py
@@ -253,9 +253,17 @@
     dp = lax.axis_index("dp")
     points = x_ref.shape[1]
     modes = weight_ref.shape[1]
-    peers = [lax.rem(me + i, n) for i in range(n)]
-    order = list(range(1, n))
-
+    peers = [me ^ i for i in range(n)]
+    order = list(range(n - 1, 0, -1))
+
+    barrier = pltpu.get_barrier_semaphore()
+    for i in order:
+        pl.semaphore_signal(
+            barrier, inc=1, device_id={"space": peers[i]}, device_id_type=pl.DeviceIdType.MESH
+        )
+    pl.semaphore_signal(
+        barrier, inc=1, device_id={"dp": 1 - dp}, device_id_type=pl.DeviceIdType.MESH
+    )
     loads = [
         pltpu.make_async_copy(source, target, load_sem.at[i])
         for i, (source, target) in enumerate(
@@ -272,15 +280,6 @@
     ]
     for load in loads:
         load.start()
-    barrier = pltpu.get_barrier_semaphore()
-    for i in order:
-        pl.semaphore_signal(
-            barrier, inc=1, device_id={"space": peers[i]}, device_id_type=pl.DeviceIdType.MESH
-        )
-    pl.semaphore_signal(
-        barrier, inc=1, device_id={"dp": 1 - dp}, device_id_type=pl.DeviceIdType.MESH
-    )
-
     def exchange(kind, source, target):
         copies = []
         for i in order:
@@ -345,6 +344,26 @@
 
     w_re, w_im = my_weight(0)[None], my_weight(1)[None]
 
+    def dot(a, b):
+        return jnp.dot(a, b, preferred_element_type=f32)
+
+    def apart(values):
+        cube = values.reshape(2, modes, modes, HALF)
+        return (cube[0], cube[1])
+
+    def joined(re, im):
+        rows = modes * modes
+        return jnp.concatenate(
+            [re.astype(bf16).reshape(rows, HALF), im.astype(bf16).reshape(rows, HALF)], axis=0
+        )
+
+    loads[5].wait()
+    loads[6].wait()
+    for copy in copies:
+        copy.wait_recv()
+    grid = stack_halves(x_in[...].reshape(n * points, LANES))
+    s_re, s_im = apart(dot(table[...], grid))
+
     for copy in g_copies:
         copy.wait_recv()
 
@@ -358,25 +377,6 @@
     g_re, g_im = my_gain(0), my_gain(1)
     k_re, k_im = complex_product(w_re, w_im, g_re, g_im)
 
-    def dot(a, b):
-        return jnp.dot(a, b, preferred_element_type=f32)
-
-    def apart(values):
-        cube = values.reshape(2, modes, modes, HALF)
-        return (cube[0], cube[1])
-
-    def joined(re, im):
-        rows = modes * modes
-        return jnp.concatenate(
-            [re.astype(bf16).reshape(rows, HALF), im.astype(bf16).reshape(rows, HALF)], axis=0
-        )
-
-    loads[5].wait()
-    loads[6].wait()
-    for copy in copies:
-        copy.wait_recv()
-    grid = stack_halves(x_in[...].reshape(n * points, LANES))
-    s_re, s_im = apart(dot(table[...], grid))
     f_re, f_im = complex_product(s_re, s_im, k_re, k_im)
     field = dot(turned[...], joined(f_re, f_im))
     field = side(field[: n * points], field[n * points :])
@@ -527,6 +527,7 @@
             collective_id=0, has_side_effects=True, vmem_limit_bytes=24 * 1024 * 1024
         ),
     )(*operands)
+    received = [pltpu.with_memory_space_constraint(x, pltpu.VMEM) for x in received]
     results = (
         jax.ShapeDtypeStruct((lat_dev, points, channels), bf16),
         jax.ShapeDtypeStruct((2, modes, channels), bf16),
@@ -539,6 +540,7 @@
         out_specs=(hbm, hbm, hbm),
         scratch_shapes=[pltpu.VMEM(x.shape, x.dtype) for x in results]
         + [pltpu.SemaphoreType.DMA((3,))],
+        compiler_params=pltpu.CompilerParams(vmem_limit_bytes=8 * 1024 * 1024),
     )(*received)
     return (out[None], wgrad, ggrad)
 
@@ -553,7 +555,7 @@
         and lat_dev == 2
         and zonal_gain.shape[1] == 2
         and channels == devices * HALF
-        and devices % 2 == 0
+        and devices & (devices - 1) == 0
         and modes % 16 == 0
         and points % 16 == 0
         and modes * modes * devices * points * 16 <= 8 * 1024 * 1024

time: 22.9 us -> 19.8 us (0.86)
  local copies, waits for them, and re-layouts: 1.81 us -> 0 us
  Pallas kernels: 20.3 us -> 19 us
    unnamed x6 -> x0, local copies, waits for them, and re-layouts: 1.81 us -> none
    pallas_call x1, Pallas kernels: 1.61 us -> 0.75 us  [channel_body(): pl.pallas_call(functools.partial(place_kernel, n), out_shape=results, in_...]
    pallas_call x1, Pallas kernels: 18.7 us -> 18.3 us  [channel_body(): pl.pallas_call(functools.partial(whole_kernel, n), out_shape=(pltpu.VMEM(...]
where the time goes in v3:
time: 19.8 us; the launch traced here: 19.7 us
  Pallas kernels  19 us (96%)
  between operations  0.64 us (3%)
    pallas_call x1, Pallas kernels, channel_body(): pl.pallas_call(functools.partial(whole_kernel, n), out_shape=(pltpu.VMEM(...  18.3 us
    pallas_call x1, Pallas kernels, channel_body(): pl.pallas_call(functools.partial(place_kernel, n), out_shape=results, in_...  0.75 us

profile of v3, /device:TPU:0, one launch (start us, length us, event | category | flops | bytes accessed | tf_op | source)
XLA Modules:
  0.0 19.7 jit_solution(16677194347655797132)
XLA Ops:
  0.6 18.3 %shard_map.94 = (bf16[8,32,128]{2,1,0:T(8,128)(2,1)S(1)}, bf16[8,16,128]{2,1,0:T(8,128)(2,1)S(1)}, f32[8,2,128]{2,1,0:T(2,128)S(1)}) custom-call(bf16[2,32,512]{2,1,0:T(8,128)(2,1)} %bitcast.4, bf16[2,32,512]{2,1,0:T(8,128)(2,1)} %bitcast.5, s32[1,16]{1,0:T(1,128)} %bitcast.6, bf16[2,16,512]{2,1,0:T(8,128)(2,1)} %weight_hbm.1, bf16[2,2,512]{2,1,0:T(2,128)(2,1)} %gain_hbm.1, ...), custom_call_target="tpu_custom_call" | custom-call | tf_op jit(solution)/shard_map/pallas_call | solution.py:499
  18.9 0.8 %shard_map.95 = (bf16[2,32,512]{2,1,0:T(8,128)(2,1)}, bf16[2,16,512]{2,1,0:T(8,128)(2,1)}, f32[2,2,512]{2,1,0:T(2,128)}) custom-call(bf16[8,32,128]{2,1,0:T(8,128)(2,1)S(1)} %get-tuple-element.9.y_in, bf16[8,16,128]{2,1,0:T(8,128)(2,1)S(1)} %get-tuple-element.10.w_in, f32[8,2,128]{2,1,0:T(2,128)S(1)} %get-tuple-element.11.q_in), custom_call_target="tpu_custom_call" | custom-call | tf_op jit(solution)/shard_map/pallas_call | solution.py:536

commit v4 on v3

--- a/solution.py
+++ b/solution.py
@@ -236,8 +236,6 @@
     x_in,
     cot_out,
     cot_in,
-    g_out,
-    g_in,
     y_out,
     part_out,
     part_in,
@@ -303,25 +301,24 @@
         for t in range(n // 2):
             a = first[:, t * LANES : (t + 1) * LANES]
             b = second[:, t * LANES : (t + 1) * LANES]
-            out[2 * t] = side(low(a), low(b))
-            out[2 * t + 1] = side(high(a), high(b))
+            out[2 * t, 0:points] = side(low(a), low(b))
+            out[2 * t + 1, 0:points] = side(high(a), high(b))
 
     loads[0].wait()
     split(x_ref, x_out)
     loads[1].wait()
-    for part in range(2):
-        rows = gain_ref[part].astype(f32)
-        for i in range(n):
-            c = i * HALF
-            g_out[i, part : part + 1, :] = side(
-                rows[0:1, c : c + HALF], rows[1:2, c : c + HALF]
-            )
+    rows = [gain_ref[part].astype(f32) for part in range(2)]
+    for i in range(n):
+        c = slice(i * HALF, (i + 1) * HALF)
+        x_out[i, points : points + 16, :] = jnp.concatenate(
+            [side(row[0:1, c], row[1:2, c]) for row in rows] + [jnp.zeros((14, LANES), f32)],
+            axis=0,
+        ).astype(bf16)
     pl.semaphore_wait(barrier, n)
     copies = exchange(0, x_out, x_in)
-    g_copies = exchange(1, g_out, g_in)
     loads[2].wait()
     split(cot_ref, cot_out)
-    cot_copies = exchange(2, cot_out, cot_in)
+    cot_copies = exchange(1, cot_out, cot_in)
 
     loads[3].wait()
     loads[4].wait()
@@ -361,16 +358,15 @@
     loads[6].wait()
     for copy in copies:
         copy.wait_recv()
-    grid = stack_halves(x_in[...].reshape(n * points, LANES))
+    grid = stack_halves(x_in[:, 0:points].reshape(n * points, LANES))
     s_re, s_im = apart(dot(table[...], grid))
 
-    for copy in g_copies:
-        copy.wait_recv()
+    gain_rows = [x_in[i, points : points + 16].astype(f32) for i in range(n)]
 
     def my_gain(part):
         total = jnp.zeros((modes, LANES), f32)
         for i in range(n):
-            row = jnp.broadcast_to(g_in[i, part : part + 1, :], (modes, LANES))
+            row = jnp.broadcast_to(gain_rows[i][part : part + 1], (modes, LANES))
             total = total + jnp.where(masks[i], row, 0.0)
         return (low(total) + high(total))[:, None, :]
 
@@ -391,30 +387,42 @@
     h_im = d_im * s_re - d_re * s_im
     wg_re = jnp.sum(h_re * g_re + h_im * g_im, axis=0)
     wg_im = jnp.sum(h_im * g_re - h_re * g_im, axis=0)
+    part_out[0] = side(wg_re, wg_im)
+
+    def swap(i):
+        return pltpu.make_async_remote_copy(
+            src_ref=part_out.at[i],
+            dst_ref=part_in.at[i],
+            send_sem=pair_sem.at[0, i],
+            recv_sem=pair_sem.at[1, i],
+            device_id={"dp": 1 - dp},
+            device_id_type=pl.DeviceIdType.MESH,
+        )
+
+    swaps = [swap(0), swap(1)]
+    swaps[0].start()
     gg_re = jnp.sum(h_re * w_re + h_im * w_im, axis=1)
     gg_im = jnp.sum(h_im * w_re - h_re * w_im, axis=1)
-    part_out[0] = side(wg_re, wg_im)
-    part_out[1] = side(gg_re, gg_im)
-    swap = pltpu.make_async_remote_copy(
-        src_ref=part_out,
-        dst_ref=part_in,
-        send_sem=pair_sem.at[0],
-        recv_sem=pair_sem.at[1],
-        device_id={"dp": 1 - dp},
-        device_id_type=pl.DeviceIdType.MESH,
-    )
-    swap.start()
+    twice = [side(gg_re, gg_re), side(gg_im, gg_im)]
+    part_out[1] = jnp.concatenate(
+        [
+            jnp.sum(jnp.where(masks[i], twice[part], 0.0), axis=0, keepdims=True)
+            for i in range(n)
+            for part in range(2)
+        ],
+        axis=0,
+    )
+    swaps[1].start()
 
     e_re = d_re * k_re + d_im * k_im
     e_im = d_im * k_re - d_re * k_im
     dgrid = dot(turned[...], joined(e_re, e_im))
     dgrid = side(dgrid[: n * points], dgrid[n * points :])
     y_out[...] = (cot + dgrid).astype(bf16).reshape(n, points, LANES)
-    y_copies = exchange(3, y_out, y_in)
-
-    swap.wait_recv()
+    y_copies = exchange(2, y_out, y_in)
+
+    swaps[0].wait_recv()
     both_w = (part_out[0] + part_in[0]).astype(bf16)
-    both_g = part_out[1] + part_in[1]
     w_out[...] = both_w
     w_copies = []
     for i in order:
@@ -422,8 +430,8 @@
             pltpu.make_async_remote_copy(
                 src_ref=w_out,
                 dst_ref=w_in.at[me],
-                send_sem=send_sem.at[4, i],
-                recv_sem=recv_sem.at[4, i],
+                send_sem=send_sem.at[3, i],
+                recv_sem=recv_sem.at[3, i],
                 device_id={"space": peers[i]},
                 device_id_type=pl.DeviceIdType.MESH,
             )
@@ -431,19 +439,16 @@
     for copy in w_copies:
         copy.start()
     w_in[me] = both_w
-    twice = [side(low(both_g), low(both_g)), side(high(both_g), high(both_g))]
-    for i in range(n):
-        for part in range(2):
-            q_out[i, part : part + 1, :] = jnp.sum(
-                jnp.where(masks[i], twice[part], 0.0), axis=0, keepdims=True
-            )
-    q_copies = exchange(5, q_out, q_in)
+    swaps[1].wait_recv()
+    q_out[...] = (part_out[1] + part_in[1]).reshape(n, 2, LANES)
+    q_copies = exchange(4, q_out, q_in)
 
     for group in (y_copies, w_copies, q_copies):
         for copy in group:
             copy.wait_recv()
-    swap.wait_send()
-    for group in (copies, g_copies, cot_copies, y_copies, w_copies, q_copies):
+    for swapped in swaps:
+        swapped.wait_send()
+    for group in (copies, cot_copies, y_copies, w_copies, q_copies):
         for copy in group:
             copy.wait_send()
 
@@ -484,6 +489,7 @@
     vmem = pl.BlockSpec(memory_space=pltpu.VMEM)
     hbm = pl.BlockSpec(memory_space=pltpu.HBM)
     block = pltpu.VMEM((n, points, LANES), bf16)
+    tall = pltpu.VMEM((n, points + 16, LANES), bf16)
     small = pltpu.VMEM((n, 2, LANES), f32)
     pair = pltpu.VMEM((2, modes, LANES), f32)
     operands = (
@@ -507,20 +513,18 @@
         out_specs=(vmem, vmem, vmem),
         scratch_shapes=[pltpu.VMEM(x.shape, x.dtype) for x in operands]
         + [
+            tall,
+            tall,
             block,
             block,
-            block,
-            block,
-            small,
-            small,
             block,
             pair,
             pair,
             pltpu.VMEM((modes, LANES), bf16),
             small,
-            pltpu.SemaphoreType.DMA((6, n)),
-            pltpu.SemaphoreType.DMA((6, n)),
-            pltpu.SemaphoreType.DMA((2,)),
+            pltpu.SemaphoreType.DMA((5, n)),
+            pltpu.SemaphoreType.DMA((5, n)),
+            pltpu.SemaphoreType.DMA((2, 2)),
             pltpu.SemaphoreType.DMA((len(operands),)),
         ],
         compiler_params=pltpu.CompilerParams(

time: 19.8 us -> 19.8 us (level)
  no operation moved by 1% of the time
where the time goes in v4:
time: 19.8 us; the launch traced here: 19.7 us
  Pallas kernels  19 us (96%)
  between operations  0.64 us (3%)
    pallas_call x1, Pallas kernels, channel_body(): pl.pallas_call(functools.partial(whole_kernel, n), out_shape=(pltpu.VMEM(...  18.3 us
    pallas_call x1, Pallas kernels, channel_body(): pl.pallas_call(functools.partial(place_kernel, n), out_shape=results, in_...  0.75 us

profile of v4, /device:TPU:0, one launch (start us, length us, event | category | flops | bytes accessed | tf_op | source)
XLA Modules:
  0.0 19.7 jit_solution(5646600112163529905)
XLA Ops:
  0.6 18.3 %shard_map.94 = (bf16[8,32,128]{2,1,0:T(8,128)(2,1)S(1)}, bf16[8,16,128]{2,1,0:T(8,128)(2,1)S(1)}, f32[8,2,128]{2,1,0:T(2,128)S(1)}) custom-call(bf16[2,32,512]{2,1,0:T(8,128)(2,1)} %bitcast.4, bf16[2,32,512]{2,1,0:T(8,128)(2,1)} %bitcast.5, s32[1,16]{1,0:T(1,128)} %bitcast.6, bf16[2,16,512]{2,1,0:T(8,128)(2,1)} %weight_hbm.1, bf16[2,2,512]{2,1,0:T(2,128)(2,1)} %gain_hbm.1, ...), custom_call_target="tpu_custom_call" | custom-call | tf_op jit(solution)/shard_map/pallas_call | solution.py:505
  18.9 0.8 %shard_map.95 = (bf16[2,32,512]{2,1,0:T(8,128)(2,1)}, bf16[2,16,512]{2,1,0:T(8,128)(2,1)}, f32[2,2,512]{2,1,0:T(2,128)}) custom-call(bf16[8,32,128]{2,1,0:T(8,128)(2,1)S(1)} %get-tuple-element.9.y_in, bf16[8,16,128]{2,1,0:T(8,128)(2,1)S(1)} %get-tuple-element.10.w_in, f32[8,2,128]{2,1,0:T(2,128)S(1)} %get-tuple-element.11.q_in), custom_call_target="tpu_custom_call" | custom-call | tf_op jit(solution)/shard_map/pallas_call | solution.py:540
